TPU v7x, 256 devices: a whole 4x4x8 slice. The times are simulated.
256 devices in a mesh: seq: 32 (over y, x, core), tp: 8 (over z).
Axes of the slice: x: 4, y: 4, z: 8, core: 2. Of those that a mesh axis runs over, the one named last changes fastest.
Arguments:
- queries: bfloat16 [32768, 5120], P('seq', 'tp'), may hold values from -120 to 120
- key_heads: bfloat16 [32768, 1024], P('seq', 'tp'), may hold values from -5 to 5
- token_value_heads: bfloat16 [32768, 1024], P('seq', 'tp'), may hold values from -6 to 6
- out_weight: bfloat16 [5120, 5120], P('tp'), may hold values from -0.078125 to 0.078125
- doc_lengths: int32 [8, 12], replicated, may hold values from 1 to 2048, 4096 in all within a row
- owner_of: int32 [256], replicated, may hold values from 0 to 31, as said below
Outputs:
- mixed: bfloat16 [32768, 5120], P('seq', 'tp')
Inputs may be any that keep to these rules, and one draw needn't show every extreme that they name: `doc_lengths`: each row holds the lengths of its 12 documents in order, summing to 4096; the longest is exactly 2048. `owner_of`: an arbitrary placement of blocks, independent of the documents. For each b in 0..7 the blocks b of the 32 indices go to 32 different owners, so every owner holds exactly one block of each b; the 8 blocks of one index go to 8 different owners.
All inputs are finite; a program needn't handle non-finite values.
Results may differ from a plain program's by a relative error of at most 0.017.
Values may be sent and summed in bfloat16 or wider, within the bound.
A program may use at most 256 MiB of HBM per device.

v0:
```python
import math

import jax
import jax.numpy as jnp
from jax import lax
from jax.sharding import PartitionSpec as P

HEAD_SIZE = 128
BLK = 128
LEN = 4096
MAXDOC = 2048


floor_score = -1e30


def shifted(shard, axis, by):
    devices = lax.axis_size(axis)
    pairs = [(i, i + by) for i in range(devices) if 0 <= i + by < devices]
    return lax.ppermute(shard, axis, pairs)


def doc_ids(doc_lengths, positions):
    seq_count, doc_count = doc_lengths.shape
    sequence_id = positions // LEN
    inner_pos = positions - sequence_id * LEN
    doc_bounds = jnp.cumsum(doc_lengths, axis=1)
    chosen = (sequence_id[:, None] == jnp.arange(seq_count, dtype=jnp.int32)[None, :]).astype(
        jnp.int32
    )
    row_bounds = jnp.sum(chosen[:, :, None] * doc_bounds[None, :, :], axis=1)
    docs_before = jnp.sum((inner_pos[:, None] >= row_bounds).astype(jnp.int32), axis=1)
    return sequence_id * doc_count + docs_before


def attend_piece(
    running,
    query_block,
    query_ids,
    query_pos,
    key_block,
    value_block,
    key_ids,
    key_pos,
    score_scale,
):
    running_max, running_sum, weighted = running
    scores = (
        jnp.einsum("qhgd,khd->hgqk", query_block, key_block, preferred_element_type=jnp.float32)
        * score_scale
    )
    allowed = (
        (query_ids[:, None] == key_ids[None, :])
        & (key_pos[None, :] <= query_pos[:, None])
        & (key_pos[None, :] >= 0)
    )
    scores = jnp.where(allowed[None, None], scores, floor_score)
    new_max = jnp.maximum(running_max, jnp.max(scores, axis=-1))
    weights = jnp.where(allowed[None, None], jnp.exp(scores - new_max[..., None]), 0.0)
    factor = jnp.exp(running_max - new_max)
    running_sum = running_sum * factor + jnp.sum(weights, axis=-1)
    weighted = weighted * factor[..., None] + jnp.einsum(
        "hgqk,khd->hgqd",
        weights.astype(jnp.bfloat16),
        value_block,
        preferred_element_type=jnp.float32,
    )
    return (new_max, running_sum, weighted)


def fold_blocks(
    running,
    query_blocks,
    query_ids,
    query_pos,
    key_block,
    value_block,
    key_ids,
    key_pos,
    score_scale,
):

    def one_block(block_index, carry_in):
        current = tuple(
            (
                lax.dynamic_index_in_dim(member, block_index, 0, keepdims=False)
                for member in carry_in
            )
        )
        query_block = lax.dynamic_index_in_dim(query_blocks, block_index, 0, keepdims=False)
        block_ids = lax.dynamic_index_in_dim(query_ids, block_index, 0, keepdims=False)
        block_pos = lax.dynamic_index_in_dim(query_pos, block_index, 0, keepdims=False)
        active = (
            (key_ids[0] <= block_ids[-1])
            & (key_ids[-1] >= block_ids[0])
            & (key_pos[0] <= block_pos[-1])
            & (key_pos[-1] >= 0)
        )
        updated = lax.cond(
            active,
            lambda inner_carry: attend_piece(
                inner_carry,
                query_block,
                block_ids,
                block_pos,
                key_block,
                value_block,
                key_ids,
                key_pos,
                score_scale,
            ),
            lambda inner_carry: inner_carry,
            current,
        )
        return tuple(
            (
                lax.dynamic_update_index_in_dim(member, fresh, block_index, 0)
                for member, fresh in zip(carry_in, updated)
            )
        )

    return lax.fori_loop(0, query_blocks.shape[0], one_block, running)


def finish(running, feature_width):
    running_max, running_sum, weighted = running
    result = weighted / running_sum[..., None]
    block_total = result.shape[0]
    block_rows = result.shape[3]
    return (
        jnp.transpose(result, (0, 3, 1, 2, 4))
        .reshape(block_total, block_rows, feature_width)
        .astype(jnp.bfloat16)
    )


def to_peers(block_data, owners_row, seq_devices):
    block_total = block_data.shape[0]
    pair_slots = -(-block_total // seq_devices)
    block_index = jnp.arange(block_total, dtype=jnp.int32)
    peer_ids = jnp.arange(seq_devices, dtype=jnp.int32)
    rounds = jnp.arange(pair_slots, dtype=jnp.int32)
    chosen = (owners_row[None, None, :] == peer_ids[:, None, None]) & (
        (block_index // seq_devices)[None, None, :] == rounds[None, :, None]
    )
    return jnp.einsum(
        "prb,bqc->prqc", chosen.astype(jnp.bfloat16), block_data, preferred_element_type=jnp.float32
    ).astype(jnp.bfloat16)


def from_peers(arrived, owner_table, device):
    seq_devices, pair_slots = (arrived.shape[0], arrived.shape[1])
    block_total = owner_table.shape[1]
    block_index = jnp.arange(block_total, dtype=jnp.int32)
    rounds = jnp.arange(pair_slots, dtype=jnp.int32)
    chosen = (jnp.transpose(owner_table)[:, :, None] == device) & (
        (block_index // seq_devices)[:, None, None] == rounds[None, None, :]
    )
    block_data = jnp.einsum(
        "bkr,krqc->bqc", chosen.astype(jnp.bfloat16), arrived, preferred_element_type=jnp.float32
    ).astype(jnp.bfloat16)
    home_ids = jnp.sum(
        jnp.where(chosen, jnp.arange(seq_devices, dtype=jnp.int32)[None, :, None], 0), axis=(1, 2)
    )
    return (block_data, home_ids)


def body(queries, key_heads, token_value_heads, out_weight, doc_lengths, owner_of):
    seq_devices = lax.axis_size("seq")
    device = lax.axis_index("seq")
    tokens_here, feature_width = queries.shape
    kv_width = key_heads.shape[1]
    kv_count = kv_width // HEAD_SIZE
    group_size = feature_width // kv_width
    block_total = tokens_here // BLK
    score_scale = 1.0 / math.sqrt(HEAD_SIZE)
    owner_table = owner_of.reshape(seq_devices, block_total)
    owners_row = lax.dynamic_index_in_dim(owner_table, device, 0, keepdims=False)
    initial = (
        jnp.full((block_total, kv_count, group_size, BLK), floor_score, jnp.float32),
        jnp.zeros((block_total, kv_count, group_size, BLK), jnp.float32),
        jnp.zeros((block_total, kv_count, group_size, BLK, HEAD_SIZE), jnp.float32),
    )

    def make_step(query_blocks, query_ids, query_pos):

        def fold_step(running, pieces, offset):
            keys_piece, values_piece = pieces
            piece_rows = keys_piece.shape[0]
            key_pos = offset + jnp.arange(piece_rows, dtype=jnp.int32)
            key_ids = doc_ids(doc_lengths, key_pos)
            return fold_blocks(
                running,
                query_blocks,
                query_ids,
                query_pos,
                keys_piece.reshape(piece_rows, kv_count, HEAD_SIZE),
                values_piece.reshape(piece_rows, kv_count, HEAD_SIZE),
                key_ids,
                key_pos,
                score_scale,
            )

        return fold_step

    query_pos = (device * tokens_here + jnp.arange(tokens_here, dtype=jnp.int32)).reshape(
        block_total, BLK
    )
    query_ids = doc_ids(doc_lengths, query_pos.reshape(-1)).reshape(block_total, BLK)
    query_blocks = queries.reshape(block_total, BLK, kv_count, group_size, HEAD_SIZE)
    fold_step = make_step(query_blocks, query_ids, query_pos)
    running = fold_step(initial, (key_heads, token_value_heads), device * tokens_here)
    joined = jnp.concatenate([key_heads, token_value_heads], axis=1)
    steps_back = min((MAXDOC - 2 + tokens_here) // tokens_here, seq_devices - 1)
    for distance in range(1, steps_back + 1):
        earlier = shifted(joined, "seq", distance)
        running = fold_step(
            running,
            (earlier[:, :kv_width], earlier[:, kv_width:]),
            (device - distance) * tokens_here,
        )
    attended = finish(running, feature_width)
    arrived = lax.all_to_all(
        to_peers(attended, owners_row, seq_devices), "seq", split_axis=0, concat_axis=0, tiled=True
    )
    placed_blocks, home_ids = from_peers(arrived, owner_table, device)
    placed = placed_blocks.reshape(tokens_here, feature_width)
    partial_value = jnp.dot(placed, out_weight, preferred_element_type=jnp.float32)
    return lax.psum_scatter(
        partial_value.astype(jnp.bfloat16), "tp", scatter_dimension=1, tiled=True
    )


def solution(mesh):
    return jax.shard_map(
        body,
        mesh=mesh,
        in_specs=(P("seq", "tp"), P("seq", "tp"), P("seq", "tp"), P("tp", None), P(), P()),
        out_specs=P("seq", "tp"),
        check_vma=False,
    )
```

profile of v0, /device:TPU:2, one launch (start us, length us, event | category | flops | bytes accessed | tf_op | source)
XLA Modules:
  0.0 501.5 jit_solution(7538797698940695261)
XLA Ops:
  26.2 81.9 %while.54 = (s32[]{:T(128)}, f32[8,1,5,128]{3,2,1,0:T(8,128)S(1)}, f32[8,1,5,128]{3,2,1,0:T(8,128)S(1)}, f32[8,1,5,128,128]{4,3,2,1,0:T(8,128)S(1)}, s32[1024]{0...) while((s32[]{:T(128)}, f32[8,1,5,128]{3,2,1,0:T(8,128)S(1)}, ...), condition=%wide.region_8.9_spmd, body=%wide.region_3.8_spmd.sunk | while | flops 344755072 | bytes 12174746 | solution.py:122
  32.7 3.7 conditional.6
  42.9 3.7 conditional.6
  53.1 3.7 conditional.6
  63.4 3.7 conditional.6
  73.6 3.7 conditional.6
  83.9 3.7 conditional.6
  94.1 3.7 conditional.6
  104.3 3.7 conditional.6
  110.0 74.6 %while.55 = (s32[]{:T(128)}, f32[8,1,5,128]{3,2,1,0:T(8,128)S(1)}, f32[8,1,5,128]{3,2,1,0:T(8,128)S(1)}, f32[8,1,5,128,128]{4,3,2,1,0:T(8,128)S(1)}, s32[1024]{0...) while((s32[]{:T(128)}, f32[8,1,5,128]{3,2,1,0:T(8,128)S(1)}, ...), condition=%wide.region_16.17_spmd, body=%wide.region_11.16_spmd.sunk | while | flops 344755072 | bytes 12174746 | solution.py:122
  116.0 3.7 conditional.7
  125.8 3.7 conditional.7
  135.6 3.7 conditional.7
  145.3 3.7 conditional.7
  155.1 3.7 conditional.7
  164.9 3.7 conditional.7
  174.7 3.7 conditional.7
  186.3 77.4 %while.56 = (s32[]{:T(128)}, f32[8,1,5,128]{3,2,1,0:T(8,128)S(1)}, f32[8,1,5,128]{3,2,1,0:T(8,128)S(1)}, f32[8,1,5,128,128]{4,3,2,1,0:T(8,128)S(1)}, s32[1024]{0...) while((s32[]{:T(128)}, f32[8,1,5,128]{3,2,1,0:T(8,128)S(1)}, ...), condition=%wide.region_24.25_spmd, body=%wide.region_19.24_spmd.sunk | while | flops 344755072 | bytes 12174746 | solution.py:122
  192.7 3.7 conditional.8
  202.8 3.7 conditional.8
  213.0 3.7 conditional.8
  223.1 3.7 conditional.8
  233.2 3.7 conditional.8
  243.4 3.7 conditional.8
  253.5 3.7 conditional.8
  271.4 4.2 copy.45
  275.6 4.7 all-to-all-start
  280.4 61.9 %all-to-all-done = bf16[32,1,128,640]{3,2,1,0:T(8,128)(2,1)} async-done(((bf16[32,1,128,640]{3,2,1,0:T(8,128)(2,1)}), bf16[32,1,128,640]{3,2,1,0:T(8,128)(2,1)}, u32[]{:S(2)}, u32[]{:S(2)}) %all-to-all-start) | async-done | bytes 5242912 | tf_op jit(solution)/shard_map/all_to_all | solution.py:223
  342.3 6.0 %fusion.90 = bf16[8,128,640]{2,0,1:T(8,128)(2,1)S(1)} fusion(bf16[32,1,128,640]{3,2,1,0:T(8,128)(2,1)} %all-to-all-done, s32[32,8]{0,1:T(8,128)S(1)} %copy.37, s32[]{:T(128)S(6)} %axis_index.15, pred[8]{0:T(512)(128)(4,1)S(1)} %fusion.119), kind=kOutput, calls=%fused_computation.117 | convolution fusion | flops 42598912 | bytes 6554636 | tf_op jit(solution)/shard_map/bkr,krqc->bqc/dot_general | solution.py:159
  348.4 13.3 %convolution_convert_fusion = bf16[1024,5120]{1,0:T(8,128)(2,1)} fusion(bf16[1024,640]{1,0:T(8,128)(2,1)S(1)} %bitcast.382, bf16[640,5120]{1,0:T(8,128)(2,1)} %param.21), kind=kOutput, calls=%fused_computation.111 | convolution fusion | flops 6716129280 | bytes 18350080 | tf_op jit(solution)/shard_map/dot_general | solution.py:228
  361.8 14.4 %copy.48 = bf16[1024,5120]{0,1:T(8,128)(2,1)} copy(bf16[1024,5120]{1,0:T(8,128)(2,1)} %convolution_convert_fusion) | data formatting | bytes 20971520
  376.2 116.1 %reduce-scatter.4.cloned.1.call-done = bf16[640,1024]{1,0:T(8,128)(2,1)} async-done(((bf16[5120,1024]{1,0:T(8,128)(2,1)}), bf16[640,1024]{1,0:T(8,128)(2,1)}) %reduce-scatter.4.cloned.1.call-update) | async-done | bytes 1310736
  (490 shorter events, 171.6 us)
Async XLA Ops:
  9.9 174.6 %collective-permute-start.1 = (bf16[1024,256]{1,0:T(8,128)(2,1)}, bf16[1024,256]{1,0:T(8,128)(2,1)}, u32[]{:S(2)}, u32[]{:S(2)}) collective-permute-start(bf16[1024,256]{1,0:T(8,128)(2,1)} %constant_dynamic-update-slice_fusion.9), channel_id=1, source_target_pairs={{0,16},{8,24},{16,32},{24,40},{32,48},{40,56},{48,64},{56,72},{64,... | collective-permute-start | bytes 1572872 | tf_op jit(solution)/shard_map/ppermute | solution.py:20
  13.3 94.9 %collective-permute-start = (bf16[1024,256]{1,0:T(8,128)(2,1)}, bf16[1024,256]{1,0:T(8,128)(2,1)}, u32[]{:S(2)}, u32[]{:S(2)}) collective-permute-start(bf16[1024,256]{1,0:T(8,128)(2,1)} %constant_dynamic-update-slice_fusion.9), channel_id=1, source_target_pairs={{0,8},{8,16},{16,24},{24,32},{32,40},{40,48},{48,56},{56,64},{64,7... | collective-permute-start | bytes 1572872 | tf_op jit(solution)/shard_map/ppermute | solution.py:20
  24.4 1.8 copy-start
  32.9 2.6 copy-start.1
  43.1 2.6 copy-start.1
  53.4 2.6 copy-start.1
  63.6 2.6 copy-start.1
  73.8 2.6 copy-start.1
  84.1 2.6 copy-start.1
  94.3 2.6 copy-start.1
  104.6 2.6 copy-start.1
  116.2 2.6 copy-start.3
  126.0 2.6 copy-start.3
  135.8 2.6 copy-start.3
  145.6 2.6 copy-start.3
  155.3 2.6 copy-start.3
  165.1 2.6 copy-start.3
  174.9 2.6 copy-start.3
  192.9 2.6 copy-start.2
  203.0 2.6 copy-start.2
  213.2 2.6 copy-start.2
  223.3 2.6 copy-start.2
  233.4 2.6 copy-start.2
  243.6 2.6 copy-start.2
  253.7 2.6 copy-start.2
  275.6 66.7 %all-to-all-start = ((bf16[32,1,128,640]{3,2,1,0:T(8,128)(2,1)}), bf16[32,1,128,640]{3,2,1,0:T(8,128)(2,1)}, u32[]{:S(2)}, u32[]{:S(2)}) async-start(bf16[32,1,128,640]{3,2,1,0:T(8,128)(2,1)} %copy.45), calls=%async_computation | async-start | bytes 10485760 | tf_op jit(solution)/shard_map/all_to_all | solution.py:223
  280.3 212.0 %reduce-scatter.4.cloned.1.call-start = ((), (), s32[]{:S(2)}) async-start(), calls=%async_computation.2 | async-start | bytes 11796480
Sparse Core Ops, SparseCore 0:
  376.3 115.9 reduce-scatter.3
where the time goes:
time: 505 us; the launch traced here: 502 us
  waiting for transfers between devices  178 us (35%)
  local copies, waits for them, and re-layouts  99.3 us (20%)
  loops' own time  93.8 us (19%)
  matrix products  77.1 us (15%)
  other arithmetic  27.7 us (5%)
  between operations  15.6 us (3%)
  starting transfers between devices  10 us (2%)
    unnamed x2, waiting for transfers between devices  116 us
    another operation x3, loops' own time, fold_blocks(): return lax.fori_loop(0, query_blocks.shape[0], one_block, running)  92.6 us
    all_to_all x1, waiting for transfers between devices, body(): lax.all_to_all(to_peers(attended, owners_row, seq_devices), 'seq', split_...  61.9 us
    dot_general x22, matrix products, attend_piece(): jnp.einsum('qhgd,khd->hgqk', query_block, key_block, preferred_element_ty...  35.9 us
    dot_general x22, matrix products, attend_piece(): jnp.einsum('hgqk,khd->hgqd', weights.astype(jnp.bfloat16), value_block, p...  19.8 us
    reduce_sum x22, other arithmetic, attend_piece(): running_sum = running_sum * factor + jnp.sum(weights, axis=-1)  19.5 us
    unnamed x5, local copies, waits for them, and re-layouts  18.5 us
    slice x24, local copies, waits for them, and re-layouts, one_block(): block_ids[0]  15.1 us
  transfers between devices with their start and end apart: 4, of which 2 were waited for; matrix products, arithmetic and copies ran while one was open for 21% of the time, Pallas kernels for 0%

commit v1 on v0

v1 whole, which is shorter than its diff:
```python
import functools
import math

import jax
import jax.numpy as jnp
from jax import lax
from jax.experimental import pallas as pl
from jax.experimental.pallas import tpu as pltpu
from jax.sharding import PartitionSpec as P

HEAD_SIZE = 128
BLK = 128
LEN = 4096
MAXDOC = 2048
HEADS = 5
ROWS = 1024
WIDTH = HEADS * HEAD_SIZE
BLOCKS = ROWS // BLK
WINDOW = MAXDOC + BLK
SEQ = 32
TP = 8
PER_SEQ = LEN // ROWS
QUARTER = BLK // 4
X_ROWS = 384
X_PIECE = 48
Y_PIECE = 32
MESH = pl.DeviceIdType.MESH

D_PROJ = 4
D_FAR = 5
D_FINAL = 7
D_MID = 9


def pair_of(z):
    return lax.rem(z + jnp.where(lax.rem(z, 2) == 1, 1, TP - 1), TP)


def buddy_of(z):
    return z + 1 - 2 * lax.rem(z, 2)


def far_of(z):
    return lax.rem(z + jnp.where(lax.rem(z, 2) == 1, 3, 5), TP)


def slot_column(z, slot):
    base = jnp.where(slot >= 2, buddy_of(z), z)
    return jnp.where(lax.rem(slot, 2) == 1, far_of(base), base)


def middle_of(block, quarter):
    return (quarter * 4 + lax.rem(block + quarter, 4)) * 2 + block // 4


def kernel(
    doc_ref,
    inverse_ref,
    q_ref,
    k_hbm,
    v_hbm,
    w_hbm,
    out_ref,
    kbuf,
    vbuf,
    weight,
    att,
    part,
    brecv,
    fsend,
    frecv,
    mixed,
    midr,
    mids,
    local_sem,
    kv_send,
    kv_recv,
    w_send,
    w_recv,
    pair_send,
    pair_recv,
    buddy_send,
    buddy_recv,
    far_send,
    far_recv,
    route_send,
    mid_recv,
    mid_send,
    out_recv,
):
    me = lax.axis_index("seq")
    z = lax.axis_index("tp")
    core = lax.rem(me, 2)
    x = lax.rem(me // 2, 4)
    y = me // 8
    j = lax.rem(me, PER_SEQ)
    pair, buddy, far = pair_of(z), buddy_of(z), far_of(z)
    scale = math.log2(math.e) / math.sqrt(HEAD_SIZE)

    def remote(src, dst, send, recv, target):
        return pltpu.make_async_remote_copy(
            src_ref=src,
            dst_ref=dst,
            send_sem=send,
            recv_sem=recv,
            device_id=target,
            device_id_type=MESH,
        )

    own_k = pltpu.make_async_copy(k_hbm, kbuf.at[pl.ds(2 * ROWS, ROWS)], local_sem.at[0])
    own_v = pltpu.make_async_copy(v_hbm, vbuf.at[pl.ds(2 * ROWS, ROWS)], local_sem.at[1])
    own_k.start()
    own_v.start()

    def own_weight(slot):
        column = pl.multiple_of(slot_column(z, slot) * WIDTH, WIDTH)
        return pltpu.make_async_copy(
            w_hbm.at[:, pl.ds(column, WIDTH)],
            weight.at[pl.ds(0, WIDTH), pl.ds(slot * WIDTH, WIDTH)],
            local_sem.at[2 + slot],
        )

    for slot in range(4):
        own_weight(slot).start()

    barrier = pltpu.get_barrier_semaphore()

    @pl.loop(1, SEQ)
    def _(step):
        pl.semaphore_signal(
            barrier, inc=1, device_id={"seq": lax.rem(me + step, SEQ)}, device_id_type=MESH
        )

    for target in (pair, buddy, far):
        pl.semaphore_signal(barrier, inc=1, device_id={"tp": target}, device_id_type=MESH)
    pl.semaphore_wait(barrier, SEQ - 1 + 3)

    rp = core * 4 + x

    def x_rows(which):
        return pl.ds(pl.multiple_of(WIDTH + which * X_PIECE, 16), X_PIECE)

    def y_rows(which):
        return pl.ds(pl.multiple_of(WIDTH + X_ROWS + which * Y_PIECE, 16), Y_PIECE)

    def slot_cols(which):
        return pl.ds(pl.multiple_of(which * WIDTH, WIDTH), WIDTH)

    theirs = pl.ds(pl.multiple_of(slot_column(pair, y) * WIDTH, WIDTH), WIDTH)

    def w_first(part_no):
        if part_no == 0:
            src = w_hbm.at[pl.ds(pl.multiple_of(rp * X_PIECE, 16), X_PIECE), theirs]
            dst = weight.at[x_rows(rp), slot_cols(y)]
        else:
            src = w_hbm.at[pl.ds(pl.multiple_of(X_ROWS + rp * Y_PIECE, 16), Y_PIECE), theirs]
            dst = weight.at[y_rows(rp), slot_cols(y)]
        return remote(src, dst, w_send.at[part_no], w_recv.at[part_no], {"tp": pair})

    def along_x(step):
        return {"seq": (y * 4 + lax.rem(x + step, 4)) * 2 + core}

    def along_y(step):
        return {"seq": (lax.rem(y + step, 4) * 4 + x) * 2 + core}

    def w_second(part_no, step):
        sem = 2 + part_no * 3 + step - 1
        if part_no == 0:
            ref, target = weight.at[x_rows(rp), slot_cols(y)], along_x(step)
        else:
            ref, target = weight.at[y_rows(rp), slot_cols(y)], along_y(step)
        return remote(ref, ref, w_send.at[sem], w_recv.at[sem], target)

    def w_third(part_no, step):
        sem = 8 + part_no * 3 + step - 1
        if part_no == 0:
            rows = pl.ds(pl.multiple_of(WIDTH + core * 4 * X_PIECE, 16), 4 * X_PIECE)
            ref, target = weight.at[rows, slot_cols(y)], along_y(step)
        else:
            ref, target = weight.at[y_rows(rp), :], along_x(step)
        return remote(ref, ref, w_send.at[sem], w_recv.at[sem], target)

    def w_fourth(part_no):
        sem = 14 + part_no
        if part_no == 0:
            rows = pl.ds(pl.multiple_of(WIDTH + core * 4 * X_PIECE, 16), 4 * X_PIECE)
        else:
            rows = pl.ds(pl.multiple_of(WIDTH + X_ROWS + core * 4 * Y_PIECE, 16), 4 * Y_PIECE)
        ref = weight.at[rows, :]
        return remote(ref, ref, w_send.at[sem], w_recv.at[sem], {"seq": me + 1 - 2 * core})

    w_first(0).start()
    w_first(1).start()

    def near_kv(which):
        src, buf = ((k_hbm, kbuf), (v_hbm, vbuf))[which]
        return remote(
            src,
            buf.at[pl.ds(ROWS, ROWS)],
            kv_send.at[which, BLOCKS],
            kv_recv.at[which, BLOCKS],
            {"seq": lax.rem(me + 1, SEQ)},
        )

    def next_kv(which, piece):
        src, buf = ((k_hbm, kbuf), (v_hbm, vbuf))[which]
        rows = pl.ds(pl.multiple_of(piece * BLK, BLK), BLK)
        return remote(
            src.at[rows],
            buf.at[rows],
            kv_send.at[which, piece],
            kv_recv.at[which, piece],
            {"seq": lax.rem(me + 2, SEQ)},
        )

    @pl.when(j < 3)
    def _():
        near_kv(0).start()
        near_kv(1).start()

    @pl.when(j < 2)
    def _():
        @pl.loop(0, BLOCKS)
        def _(step):
            next_kv(0, BLOCKS - 1 - step).start()
            next_kv(1, BLOCKS - 1 - step).start()

        kbuf[pl.ds(0, ROWS), :] = jnp.zeros((ROWS, HEAD_SIZE), kbuf.dtype)
        vbuf[pl.ds(0, ROWS), :] = jnp.zeros((ROWS, HEAD_SIZE), vbuf.dtype)

    @pl.when(j < 1)
    def _():
        kbuf[pl.ds(ROWS, ROWS), :] = jnp.zeros((ROWS, HEAD_SIZE), kbuf.dtype)
        vbuf[pl.ds(ROWS, ROWS), :] = jnp.zeros((ROWS, HEAD_SIZE), vbuf.dtype)

    def rows_of(block):
        return pl.ds(pl.multiple_of(block * BLK, BLK), BLK)

    def pair_copy(block):
        rows = rows_of(block)
        return remote(
            att.at[rows, pl.ds(0, WIDTH)],
            att.at[rows, pl.ds(WIDTH, WIDTH)],
            pair_send.at[block],
            pair_recv.at[block],
            {"tp": pair},
        )

    def buddy_copy(block):
        rows = rows_of(block)
        return remote(
            part.at[rows, pl.ds(2 * WIDTH, 2 * WIDTH)],
            brecv.at[rows],
            buddy_send.at[block],
            buddy_recv.at[block],
            {"tp": buddy},
        )

    def far_copy(block):
        rows = rows_of(block)
        return remote(
            fsend.at[rows], frecv.at[rows], far_send.at[block], far_recv.at[block], {"tp": far}
        )

    def attention(block):
        rows = rows_of(block)
        window = pl.ds(pl.multiple_of(block * BLK, BLK), WINDOW)
        keys = kbuf[window, :]
        values = vbuf[window, :]
        base = j * ROWS + block * BLK
        position = base + lax.broadcasted_iota(jnp.int32, (BLK, 1), 0)
        bound = jnp.int32(0)
        first = jnp.zeros((BLK, 1), jnp.int32)
        for doc in range(doc_ref.shape[1]):
            bound = bound + doc_ref[me // PER_SEQ, doc]
            first = jnp.where(position >= bound, bound, first)
        first = first - base + MAXDOC
        key_no = lax.broadcasted_iota(jnp.int32, (BLK, WINDOW), 1)
        last = MAXDOC + lax.broadcasted_iota(jnp.int32, (BLK, WINDOW), 0)
        allowed = (key_no >= first) & (key_no <= last)
        for head in range(HEADS):
            columns = pl.ds(head * HEAD_SIZE, HEAD_SIZE)
            scores = lax.dot_general(
                q_ref[rows, columns],
                keys,
                (((1,), (1,)), ((), ())),
                preferred_element_type=jnp.float32,
            )
            scores = jnp.where(allowed, scores * scale, -1e30)
            weights = jnp.exp2(scores - jnp.max(scores, axis=1, keepdims=True))
            total = jnp.sum(weights, axis=1, keepdims=True)
            mix = jnp.dot(
                weights.astype(jnp.bfloat16), values, preferred_element_type=jnp.float32
            )
            att[rows, columns] = (mix / total).astype(jnp.bfloat16)

    def project(block, slots):
        rows = rows_of(block)
        for slot in slots:
            columns = pl.ds(slot * WIDTH, WIDTH)
            part[rows, columns] = jnp.dot(
                att[rows, :], weight[:, columns], preferred_element_type=jnp.float32
            ).astype(jnp.bfloat16)

    def route_copy(block, quarter, target):
        rows = pl.ds(pl.multiple_of(block * BLK + quarter * QUARTER, QUARTER), QUARTER)
        return remote(
            mixed.at[rows], midr.at[me], route_send.at[block, quarter], mid_recv, {"seq": target}
        )

    my_quarter = y
    my_block = core * 4 + lax.rem(x + 4 - y, 4)
    my_rows = pl.ds(pl.multiple_of(my_block * BLK + my_quarter * QUARTER, QUARTER), QUARTER)

    def mid_copy(target):
        return remote(
            mids.at[target],
            out_ref.at[my_rows],
            mid_send.at[target],
            out_recv.at[my_block],
            {"seq": target},
        )

    own_mid = pltpu.make_async_copy(mixed.at[my_rows], midr.at[me], mid_recv)
    own_out = pltpu.make_async_copy(mids.at[me], out_ref.at[my_rows], out_recv.at[my_block])

    @pl.loop(0, BLOCKS + D_MID)
    def _(step):
        @pl.when(step == 0)
        def _():
            own_k.wait()
            own_v.wait()

            @pl.when(j >= 1)
            def _():
                near_kv(0).wait_recv()
                near_kv(1).wait_recv()

        @pl.when(step == 1)
        def _():
            for no in range(2):
                w_first(no).wait_recv()
                for hop in (1, 3, 2):
                    w_second(no, hop).start()

        @pl.when(step == 2)
        def _():
            for no in range(2):
                for hop in (1, 3, 2):
                    w_second(no, hop).wait_recv()
                for hop in (1, 3, 2):
                    w_third(no, hop).start()

        @pl.when(step == 3)
        def _():
            for no in range(2):
                for hop in (1, 3, 2):
                    w_third(no, hop).wait_recv()
                w_fourth(no).start()

        @pl.when(step == D_PROJ)
        def _():
            for slot in range(4):
                own_weight(slot).wait()
            for no in range(2):
                w_fourth(no).wait_recv()

        @pl.when((step >= D_PROJ) & (step < D_PROJ + BLOCKS))
        def _():
            block = BLOCKS - 1 - (step - D_PROJ)
            pair_copy(block).wait_recv()
            project(block, (2, 3))
            buddy_copy(block).start()
            project(block, (1, 0))

        @pl.when((step >= D_FAR) & (step < D_FAR + BLOCKS))
        def _():
            block = BLOCKS - 1 - (step - D_FAR)
            rows = rows_of(block)
            buddy_copy(block).wait_recv()
            columns = pl.ds(WIDTH, WIDTH)
            fsend[rows, :] = (
                part[rows, columns].astype(jnp.float32) + brecv[rows, columns].astype(jnp.float32)
            ).astype(jnp.bfloat16)
            far_copy(block).start()

        @pl.when(step < BLOCKS)
        def _():
            block = BLOCKS - 1 - step

            @pl.when(j >= 2)
            def _():
                next_kv(0, block).wait_recv()
                next_kv(1, block).wait_recv()

            attention(block)
            pair_copy(block).start()

        @pl.when((step >= D_FINAL) & (step < D_FINAL + BLOCKS))
        def _():
            block = BLOCKS - 1 - (step - D_FINAL)
            rows = rows_of(block)
            far_copy(block).wait_recv()
            columns = pl.ds(0, WIDTH)
            mixed[rows, :] = (
                part[rows, columns].astype(jnp.float32)
                + brecv[rows, columns].astype(jnp.float32)
                + frecv[rows, :].astype(jnp.float32)
            ).astype(jnp.bfloat16)
            for quarter in range(4):
                target = middle_of(block, quarter)

                @pl.when(target != me)
                def _():
                    route_copy(block, quarter, target).start()

                @pl.when(target == me)
                def _():
                    own_mid.start()

        @pl.when(BLOCKS - 1 - (step - D_MID) == my_block)
        def _():
            pltpu.make_async_copy(midr, midr, mid_recv).wait()

            @pl.loop(0, SEQ)
            def _(owner):
                mids[owner] = midr[inverse_ref[my_block * SEQ + owner]]

                @pl.when(owner != me)
                def _():
                    mid_copy(owner).start()

                @pl.when(owner == me)
                def _():
                    own_out.start()

    for block in range(BLOCKS):
        rows = pl.ds(block * BLK, BLK)
        pltpu.make_async_copy(out_ref.at[rows], out_ref.at[rows], out_recv.at[block]).wait()

    @pl.when(j < 3)
    def _():
        near_kv(0).wait_send()
        near_kv(1).wait_send()

    @pl.when(j < 2)
    def _():
        @pl.loop(0, BLOCKS)
        def _(piece):
            next_kv(0, piece).wait_send()
            next_kv(1, piece).wait_send()

    for no in range(2):
        w_first(no).wait_send()
        w_fourth(no).wait_send()
        for hop in (1, 2, 3):
            w_second(no, hop).wait_send()
            w_third(no, hop).wait_send()

    @pl.loop(0, BLOCKS)
    def _(block):
        pair_copy(block).wait_send()
        buddy_copy(block).wait_send()
        far_copy(block).wait_send()
        for quarter in range(4):
            target = middle_of(block, quarter)

            @pl.when(target != me)
            def _():
                route_copy(block, quarter, target).wait_send()

    @pl.loop(0, SEQ)
    def _(owner):
        @pl.when(owner != me)
        def _():
            mid_copy(owner).wait_send()


def body(queries, key_heads, token_value_heads, out_weight, doc_lengths, owner_of):
    owner_table = owner_of.reshape(SEQ, BLOCKS)
    index = jnp.arange(SEQ, dtype=jnp.int32)
    inverse = jnp.sum(
        jnp.where(owner_table.T[:, None, :] == index[None, :, None], index[None, None, :], 0),
        axis=2,
    ).reshape(BLOCKS * SEQ)
    dma = pltpu.SemaphoreType.DMA
    bf16 = jnp.bfloat16
    any_space = pl.BlockSpec(memory_space=pl.ANY)
    smem = pl.BlockSpec(memory_space=pltpu.SMEM)
    vmem = pl.BlockSpec(memory_space=pltpu.VMEM)
    return pl.pallas_call(
        kernel,
        out_shape=jax.ShapeDtypeStruct((ROWS, WIDTH), bf16),
        in_specs=[smem, smem, vmem, any_space, any_space, any_space],
        out_specs=any_space,
        scratch_shapes=[
            pltpu.VMEM((3 * ROWS, HEAD_SIZE), bf16),
            pltpu.VMEM((3 * ROWS, HEAD_SIZE), bf16),
            pltpu.VMEM((2 * WIDTH, 4 * WIDTH), bf16),
            pltpu.VMEM((ROWS, 2 * WIDTH), bf16),
            pltpu.VMEM((ROWS, 4 * WIDTH), bf16),
            pltpu.VMEM((ROWS, 2 * WIDTH), bf16),
            pltpu.VMEM((ROWS, WIDTH), bf16),
            pltpu.VMEM((ROWS, WIDTH), bf16),
            pltpu.VMEM((ROWS, WIDTH), bf16),
            pltpu.VMEM((SEQ, QUARTER, WIDTH), bf16),
            pltpu.VMEM((SEQ, QUARTER, WIDTH), bf16),
            dma((6,)),
            dma((2, BLOCKS + 1)),
            dma((2, BLOCKS + 1)),
            dma((16,)),
            dma((16,)),
            dma((BLOCKS,)),
            dma((BLOCKS,)),
            dma((BLOCKS,)),
            dma((BLOCKS,)),
            dma((BLOCKS,)),
            dma((BLOCKS,)),
            dma((BLOCKS, 4)),
            dma,
            dma((SEQ,)),
            dma((BLOCKS,)),
        ],
        compiler_params=pltpu.CompilerParams(
            collective_id=0, has_side_effects=True, vmem_limit_bytes=56 * 1024 * 1024
        ),
        cost_estimate=pl.CostEstimate(
            flops=20_000_000_000, bytes_accessed=12_000_000, transcendentals=11_000_000
        ),
    )(doc_lengths, inverse, queries, key_heads, token_value_heads, out_weight)


def solution(mesh):
    return jax.shard_map(
        body,
        mesh=mesh,
        in_specs=(P("seq", "tp"), P("seq", "tp"), P("seq", "tp"), P("tp", None), P(), P()),
        out_specs=P("seq", "tp"),
        check_vma=False,
    )
```

time: 505 us -> 168 us (0.33)
  the two profiles are of different devices: /device:TPU:2 before, /device:TPU:63 now
where the time goes in v1:
time: 168 us
  Pallas kernels  164 us (98%)
  local copies, waits for them, and re-layouts  3.96 us (2%)
    pallas_call x1, Pallas kernels, body(): pl.pallas_call(kernel, out_shape=jax.ShapeDtypeStruct((ROWS, WIDTH), bf16...  164 us

profile of v1, /device:TPU:63, one launch (start us, length us, event | category | flops | bytes accessed | tf_op | source)
XLA Modules:
  0.0 167.8 jit_solution(6196166709699363438)
XLA Ops:
  0.0 0.8 reshape.7
  0.8 0.1 copy.9
  0.8 0.2 select_reduce_fusion
  1.1 0.6 reshape.8.inverse_ref
  1.7 163.6 %shard_map.64 = bf16[1024,640]{1,0:T(8,128)(2,1)} custom-call(s32[8,12]{1,0:T(8,128)} %doc_ref.1, s32[256]{0:T(256)} %reshape.8.inverse_ref, bf16[1024,640]{1,0:T(8,128)(2,1)} %q_ref.1, bf16[1024,128]{1,0:T(8,128)(2,1)} %k_hbm.1, bf16[1024,128]{1,0:T(8,128)(2,1)} %v_hbm.1, bf16[640,5120]{1,0:T(8,128)(2,1)} %w_hbm.1), custom_call_target="tpu_custom_call" | custom-call | flops 20000000000 | bytes 12000000 | tf_op jit(solution)/shard_map/pallas_call | solution.py:491
  165.3 2.5 %copy.11 = bf16[1024,640]{1,0:T(8,128)(2,1)} copy(bf16[1024,640]{1,0:T(8,128)(2,1)} %shard_map.64) | data formatting | bytes 2621440

commit v2 on v1

v2 whole, which is shorter than its diff:
```python
import functools
import math

import jax
import jax.numpy as jnp
from jax import lax
from jax.experimental import pallas as pl
from jax.experimental.pallas import tpu as pltpu
from jax.sharding import PartitionSpec as P

HEAD_SIZE = 128
BLK = 128
LEN = 4096
MAXDOC = 2048
HEADS = 5
ROWS = 1024
WIDTH = HEADS * HEAD_SIZE
BLOCKS = ROWS // BLK
WINDOW = MAXDOC + BLK
SEQ = 32
TP = 8
PER_SEQ = LEN // ROWS
PIECES = 8
PIECE = BLK // PIECES
W_PIECE = 64
W_ROWS = 4 * WIDTH + 128
MESH = pl.DeviceIdType.MESH

HALF = BLOCKS // 2

D_FORWARD = 2
D_PROJ = 4
D_FINAL = 5
D_MID = 6


def block_at(place):
    late = jnp.where(place == 7, 0, 13 - 2 * place)
    return jnp.where(place < HALF, jnp.where(place == 0, 7, 8 - 2 * place), late)


def pair_of(z):
    return lax.rem(z + jnp.where(lax.rem(z, 2) == 1, 1, TP - 1), TP)


def buddy_of(z):
    return z + 1 - 2 * lax.rem(z, 2)


def far_of(z):
    return lax.rem(z + jnp.where(lax.rem(z, 2) == 1, 3, 5), TP)


def middle_of(place, piece):
    y = piece // 2
    x = 2 * (piece % 2) + lax.rem(y + place, 2)
    return (y * 4 + x) * 2 + lax.rem(place // 2, 2)


def kernel(
    doc_ref,
    inverse_ref,
    q_ref,
    k_hbm,
    v_hbm,
    w_hbm,
    out_ref,
    kbuf,
    vbuf,
    weight,
    att,
    psend,
    precv,
    own_part,
    attended,
    mixed,
    midr_low,
    midr_high,
    mids,
    local_sem,
    kv_send,
    kv_recv,
    w_send,
    w_recv,
    own_send,
    own_recv,
    far_send,
    far_recv,
    forward_send,
    forward_recv,
    pair_send,
    pair_recv,
    route_send,
    mid_recv,
    mid_send,
    placed_recv,
    out_recv,
):
    midr = (midr_low, midr_high)
    me = lax.axis_index("seq")
    z = lax.axis_index("tp")
    core = lax.rem(me, 2)
    x = lax.rem(me // 2, 4)
    y = me // 8
    j = lax.rem(me, PER_SEQ)
    pair, buddy, far = pair_of(z), buddy_of(z), far_of(z)
    far_buddy = buddy_of(far)
    scale = math.log2(math.e) / math.sqrt(HEAD_SIZE)

    def remote(src, dst, send, recv, target):
        return pltpu.make_async_remote_copy(
            src_ref=src,
            dst_ref=dst,
            send_sem=send,
            recv_sem=recv,
            device_id=target,
            device_id_type=MESH,
        )

    own_k = pltpu.make_async_copy(k_hbm, kbuf.at[pl.ds(2 * ROWS, ROWS)], local_sem.at[0])
    own_v = pltpu.make_async_copy(v_hbm, vbuf.at[pl.ds(2 * ROWS, ROWS)], local_sem.at[1])
    own_k.start()
    own_v.start()

    def own_weight(half):
        column = pl.multiple_of((pair if half else z) * WIDTH, WIDTH)
        return pltpu.make_async_copy(
            w_hbm.at[:, pl.ds(column, WIDTH)],
            weight.at[pl.ds(0, WIDTH), pl.ds(half * WIDTH, WIDTH)],
            local_sem.at[2 + half],
        )

    for half in range(2):
        own_weight(half).start()

    barrier = pltpu.get_barrier_semaphore()

    @pl.loop(1, SEQ)
    def _(step):
        pl.semaphore_signal(
            barrier, inc=1, device_id={"seq": lax.rem(me + step, SEQ)}, device_id_type=MESH
        )

    for target in (pair, buddy, far, far_buddy):
        pl.semaphore_signal(barrier, inc=1, device_id={"tp": target}, device_id_type=MESH)
    pl.semaphore_wait(barrier, SEQ - 1 + 4)

    piece_no = (core * 4 + y) * 4 + x
    group = jnp.minimum(piece_no // 10, 2)
    w_target = jnp.where(group == 0, buddy, jnp.where(group == 1, far, far_buddy))

    def w_rows(yy, xx):
        start = WIDTH + ((core * 4 + yy) * 4 + xx) * W_PIECE
        return pl.ds(pl.multiple_of(start, W_PIECE), W_PIECE)

    def w_half(half):
        return pl.ds(half * WIDTH, WIDTH)

    def w_first(half):
        column = pair_of(w_target) if half else w_target
        src = w_hbm.at[
            pl.ds(pl.multiple_of(lax.rem(piece_no, 10) * W_PIECE, W_PIECE), W_PIECE),
            pl.ds(pl.multiple_of(column * WIDTH, WIDTH), WIDTH),
        ]
        dst = weight.at[w_rows(y, x), w_half(half)]
        return remote(src, dst, w_send.at[half], w_recv.at[half], {"tp": w_target})

    def along_x(hop):
        return {"seq": (y * 4 + lax.rem(x + hop, 4)) * 2 + core}

    def along_y(hop):
        return {"seq": (lax.rem(y + hop, 4) * 4 + x) * 2 + core}

    def w_second(half, hop):
        sem = 2 + half * 3 + hop - 1
        ref = weight.at[w_rows(y, x), w_half(half)]
        target = along_y(hop) if half else along_x(hop)
        return remote(ref, ref, w_send.at[sem], w_recv.at[sem], target)

    four_rows = pl.ds(pl.multiple_of(WIDTH + (core * 4 + y) * 4 * W_PIECE, W_PIECE), 4 * W_PIECE)

    def w_third(half, hop):
        sem = 8 + half * 3 + hop - 1
        ref = weight.at[four_rows, w_half(half)]
        target = along_x(hop) if half else along_y(hop)
        return remote(ref, ref, w_send.at[sem], w_recv.at[sem], target)

    def w_third_piece(hop, yy):
        sem = 11 + hop - 1
        ref = weight.at[w_rows(yy, x), w_half(1)]
        return remote(ref, ref, w_send.at[sem], w_recv.at[sem], along_x(hop))

    def w_fourth(half):
        sem = 14 + half
        rows = pl.ds(pl.multiple_of(WIDTH + core * 16 * W_PIECE, W_PIECE), 16 * W_PIECE)
        ref = weight.at[rows, w_half(half)]
        return remote(ref, ref, w_send.at[sem], w_recv.at[sem], {"seq": me + 1 - 2 * core})

    w_first(0).start()
    w_first(1).start()

    def near_kv(which):
        src, buf = ((k_hbm, kbuf), (v_hbm, vbuf))[which]
        return remote(
            src,
            buf.at[pl.ds(ROWS, ROWS)],
            kv_send.at[which, BLOCKS],
            kv_recv.at[which, BLOCKS],
            {"seq": lax.rem(me + 1, SEQ)},
        )

    def next_kv(which, piece):
        src, buf = ((k_hbm, kbuf), (v_hbm, vbuf))[which]
        rows = pl.ds(pl.multiple_of(piece * BLK, BLK), BLK)
        return remote(
            src.at[rows],
            buf.at[rows],
            kv_send.at[which, piece],
            kv_recv.at[which, piece],
            {"seq": lax.rem(me + 2, SEQ)},
        )

    @pl.when(j < 3)
    def _():
        near_kv(0).start()
        near_kv(1).start()

    @pl.when(j < 2)
    def _():
        next_kv(0, BLOCKS - 1).start()
        next_kv(1, BLOCKS - 1).start()
        kbuf[pl.ds(0, ROWS), :] = jnp.zeros((ROWS, HEAD_SIZE), kbuf.dtype)
        vbuf[pl.ds(0, ROWS), :] = jnp.zeros((ROWS, HEAD_SIZE), vbuf.dtype)

    @pl.when(j < 1)
    def _():
        kbuf[pl.ds(ROWS, ROWS), :] = jnp.zeros((ROWS, HEAD_SIZE), kbuf.dtype)
        vbuf[pl.ds(ROWS, ROWS), :] = jnp.zeros((ROWS, HEAD_SIZE), vbuf.dtype)

    def rows_of(block):
        return pl.ds(pl.multiple_of(block * BLK, BLK), BLK)

    def slot(no):
        return pl.ds(no * WIDTH, WIDTH)

    def own_copy(block):
        rows = rows_of(block)
        return remote(
            att.at[rows, slot(0)],
            att.at[rows, slot(1)],
            own_send.at[block],
            own_recv.at[block],
            {"tp": buddy},
        )

    def far_copy(block):
        rows = rows_of(block)
        return remote(
            att.at[rows, slot(0)],
            att.at[rows, slot(2)],
            far_send.at[block],
            far_recv.at[block],
            {"tp": far},
        )

    def forward_copy(block):
        rows = rows_of(block)
        return remote(
            att.at[rows, slot(2)],
            att.at[rows, slot(3)],
            forward_send.at[block],
            forward_recv.at[block],
            {"tp": buddy},
        )

    def pair_copy(block):
        rows = rows_of(block)
        return remote(
            psend.at[rows], precv.at[rows], pair_send.at[block], pair_recv.at[block], {"tp": pair}
        )

    def attention(place):
        block = block_at(place)
        rows = rows_of(block)
        window = pl.ds(pl.multiple_of(block * BLK, BLK), WINDOW)
        keys = kbuf[window, :]
        values = vbuf[window, :]
        base = j * ROWS + block * BLK
        position = base + lax.broadcasted_iota(jnp.int32, (BLK, 1), 0)
        bound = jnp.int32(0)
        first = jnp.zeros((BLK, 1), jnp.int32)
        for doc in range(doc_ref.shape[1]):
            bound = bound + doc_ref[me // PER_SEQ, doc]
            first = jnp.where(position >= bound, bound, first)
        first = first - base + MAXDOC
        key_no = lax.broadcasted_iota(jnp.int32, (BLK, WINDOW), 1)
        last = MAXDOC + lax.broadcasted_iota(jnp.int32, (BLK, WINDOW), 0)
        allowed = (key_no >= first) & (key_no <= last)
        for head in range(HEADS):
            columns = pl.ds(head * HEAD_SIZE, HEAD_SIZE)
            scores = lax.dot_general(
                q_ref[rows, columns],
                keys,
                (((1,), (1,)), ((), ())),
                preferred_element_type=jnp.float32,
            )
            scores = jnp.where(allowed, scores * scale, -1e30)
            weights = jnp.exp2(scores - jnp.max(scores, axis=1, keepdims=True))
            total = jnp.sum(weights, axis=1, keepdims=True)
            mix = jnp.dot(
                weights.astype(jnp.bfloat16), values, preferred_element_type=jnp.float32
            )
            attended[rows_of(place), columns] = (mix / total).astype(jnp.bfloat16)

    def project(block, half):
        return jnp.dot(
            att[rows_of(block), :],
            weight[pl.ds(0, 4 * WIDTH), pl.ds(half * WIDTH, WIDTH)],
            preferred_element_type=jnp.float32,
        )

    def route_copy(place, piece, role, target):
        rows = pl.ds(pl.multiple_of(place * BLK + piece * PIECE, PIECE), PIECE)
        return remote(
            (mixed, attended)[role].at[rows],
            midr[role].at[me],
            route_send.at[place, piece],
            mid_recv.at[role],
            {"seq": target},
        )

    my_piece = y * 2 + x // 2

    def my_place(role):
        return lax.rem(x + y, 2) + 2 * core + HALF * role

    def piece_rows(block):
        return pl.ds(pl.multiple_of(block * BLK + my_piece * PIECE, PIECE), PIECE)

    def mid_target(role):
        place = my_place(role)
        if role == 0:
            return out_ref.at[piece_rows(block_at(place))], out_recv.at[place]
        return att.at[piece_rows(place), slot(0)], placed_recv.at[place - HALF]

    def mid_copy(role, target):
        dst, sem = mid_target(role)
        return remote(
            mids.at[role, target], dst, mid_send.at[role, target], sem, {"seq": target}
        )

    def own_mid(role):
        src = (mixed, attended)[role].at[piece_rows(my_place(role))]
        return pltpu.make_async_copy(src, midr[role].at[me], mid_recv.at[role])

    def own_out(role):
        dst, sem = mid_target(role)
        return pltpu.make_async_copy(mids.at[role, me], dst, sem)

    def route(place, role):
        for piece in range(PIECES):
            target = middle_of(place, piece)

            @pl.when(target != me)
            def _():
                route_copy(place, piece, role, target).start()

        @pl.when(place == my_place(role))
        def _():
            own_mid(role).start()

    def reorder(place, role):
        @pl.when(place == my_place(role))
        def _():
            pltpu.make_async_copy(midr[role], midr[role], mid_recv.at[role]).wait()
            block = block_at(place)

            @pl.loop(0, SEQ)
            def _(owner):
                mids[role, owner] = midr[role][inverse_ref[block, owner]]

                @pl.when(owner != me)
                def _():
                    mid_copy(role, owner).start()

                @pl.when(owner == me)
                def _():
                    own_out(role).start()

    def placed_wait(place):
        ref = att.at[rows_of(place), slot(0)]
        pltpu.make_async_copy(ref, ref, placed_recv.at[place - HALF]).wait()

    def own_result(place):
        return pltpu.make_async_copy(
            mixed.at[rows_of(place)], out_ref.at[rows_of(block_at(place))], out_recv.at[place]
        )

    @pl.loop(0, BLOCKS + D_FINAL)
    def _(step):
        @pl.when(step == 0)
        def _():
            own_k.wait()
            own_v.wait()

            @pl.when(j >= 1)
            def _():
                near_kv(0).wait_recv()
                near_kv(1).wait_recv()

        @pl.when(step == 1)
        def _():
            for half in range(2):
                w_first(half).wait_recv()
                for hop in (1, 3, 2):
                    w_second(half, hop).start()

            @pl.when(j < 2)
            def _():
                @pl.loop(1, BLOCKS)
                def _(back):
                    next_kv(0, BLOCKS - 1 - back).start()
                    next_kv(1, BLOCKS - 1 - back).start()

        @pl.when(step == 2)
        def _():
            for half in range(2):
                for hop in (1, 3, 2):
                    w_second(half, hop).wait_recv()
            for hop in (1, 3, 2):
                w_third(0, hop).start()
                for yy in range(4):
                    w_third_piece(hop, yy).start()

        @pl.when(step == 3)
        def _():
            for half in range(2):
                for hop in (1, 3, 2):
                    w_third(half, hop).wait_recv()
                w_fourth(half).start()

        @pl.when((step >= D_FORWARD) & (step < D_FORWARD + BLOCKS))
        def _():
            place = step - D_FORWARD
            far_copy(place).wait_recv()
            forward_copy(place).start()

        @pl.when((step >= HALF) & (step < BLOCKS))
        def _():
            placed_wait(step)
            far_copy(step).start()
            own_copy(step).start()

        @pl.loop(0, 2)
        def _(late):
            place = jnp.where(late == 1, step + HALF - 1, step)
            first_step = late

            @pl.when((step >= first_step) & (step < first_step + HALF))
            def _():
                @pl.when(j >= 2)
                def _():
                    next_kv(0, block_at(place)).wait_recv()
                    next_kv(1, block_at(place)).wait_recv()

                attention(place)

                @pl.when(late == 0)
                def _():
                    rows = rows_of(place)
                    att[rows, slot(0)] = attended[rows, :]
                    far_copy(place).start()
                    own_copy(place).start()

                @pl.when(late == 1)
                def _():
                    route(place, 1)

        reorder(step + 2, 1)

        @pl.when(step == D_PROJ)
        def _():
            for half in range(2):
                own_weight(half).wait()
                w_fourth(half).wait_recv()

        @pl.when((step >= D_PROJ) & (step < D_PROJ + BLOCKS))
        def _():
            place = step - D_PROJ
            rows = rows_of(place)
            own_copy(place).wait_recv()
            forward_copy(place).wait_recv()
            psend[rows, :] = project(place, 1).astype(jnp.bfloat16)
            pair_copy(place).start()
            own_part[rows, :] = project(place, 0)

        @pl.when((step >= D_FINAL) & (step < D_FINAL + BLOCKS))
        def _():
            place = step - D_FINAL
            rows = rows_of(place)
            pair_copy(place).wait_recv()
            mixed[rows, :] = (
                own_part[rows, :] + precv[rows, :].astype(jnp.float32)
            ).astype(jnp.bfloat16)

            @pl.when(place < HALF)
            def _():
                route(place, 0)

            @pl.when(place >= HALF)
            def _():
                own_result(place).start()

        reorder(step - D_MID, 0)

    for block in range(BLOCKS):
        rows = pl.ds(block * BLK, BLK)
        pltpu.make_async_copy(out_ref.at[rows], out_ref.at[rows], out_recv.at[block]).wait()

    @pl.when(j < 3)
    def _():
        near_kv(0).wait_send()
        near_kv(1).wait_send()

    @pl.when(j < 2)
    def _():
        @pl.loop(0, BLOCKS)
        def _(piece):
            next_kv(0, piece).wait_send()
            next_kv(1, piece).wait_send()

    for half in range(2):
        w_first(half).wait_send()
        w_fourth(half).wait_send()
        for hop in (1, 2, 3):
            w_second(half, hop).wait_send()
            w_third(half, hop).wait_send()

    @pl.loop(0, BLOCKS)
    def _(block):
        own_copy(block).wait_send()
        far_copy(block).wait_send()
        forward_copy(block).wait_send()
        pair_copy(block).wait_send()
        for piece in range(PIECES):
            target = middle_of(block, piece)

            @pl.when(target != me)
            def _():
                route_copy(block, piece, 0, target).wait_send()

    @pl.loop(0, SEQ)
    def _(owner):
        @pl.when(owner != me)
        def _():
            mid_copy(0, owner).wait_send()
            mid_copy(1, owner).wait_send()


def body(queries, key_heads, token_value_heads, out_weight, doc_lengths, owner_of):
    index = jnp.arange(SEQ * BLOCKS, dtype=jnp.int32)[None, None, :]
    blocks = jnp.arange(BLOCKS, dtype=jnp.int32)[:, None, None]
    owners = jnp.arange(SEQ, dtype=jnp.int32)[None, :, None]
    inverse = jnp.sum(
        jnp.where(
            (owner_of[None, None, :] == owners) & (index % BLOCKS == blocks), index // BLOCKS, 0
        ),
        axis=2,
    )
    dma = pltpu.SemaphoreType.DMA
    bf16 = jnp.bfloat16
    any_space = pl.BlockSpec(memory_space=pl.ANY)
    smem = pl.BlockSpec(memory_space=pltpu.SMEM)
    vmem = pl.BlockSpec(memory_space=pltpu.VMEM)
    return pl.pallas_call(
        kernel,
        out_shape=jax.ShapeDtypeStruct((ROWS, WIDTH), bf16),
        in_specs=[smem, smem, vmem, any_space, any_space, any_space],
        out_specs=any_space,
        scratch_shapes=[
            pltpu.VMEM((3 * ROWS, HEAD_SIZE), bf16),
            pltpu.VMEM((3 * ROWS, HEAD_SIZE), bf16),
            pltpu.VMEM((W_ROWS, 2 * WIDTH), bf16),
            pltpu.VMEM((ROWS, 4 * WIDTH), bf16),
            pltpu.VMEM((ROWS, WIDTH), bf16),
            pltpu.VMEM((ROWS, WIDTH), bf16),
            pltpu.VMEM((ROWS, WIDTH), jnp.float32),
            pltpu.VMEM((ROWS, WIDTH), bf16),
            pltpu.VMEM((ROWS, WIDTH), bf16),
            pltpu.VMEM((SEQ, PIECE, WIDTH), bf16),
            pltpu.VMEM((SEQ, PIECE, WIDTH), bf16),
            pltpu.VMEM((2, SEQ, PIECE, WIDTH), bf16),
            dma((4,)),
            dma((2, BLOCKS + 1)),
            dma((2, BLOCKS + 1)),
            dma((16,)),
            dma((16,)),
            dma((BLOCKS,)),
            dma((BLOCKS,)),
            dma((BLOCKS,)),
            dma((BLOCKS,)),
            dma((BLOCKS,)),
            dma((BLOCKS,)),
            dma((BLOCKS,)),
            dma((BLOCKS,)),
            dma((BLOCKS, PIECES)),
            dma((2,)),
            dma((2, SEQ)),
            dma((HALF,)),
            dma((BLOCKS,)),
        ],
        compiler_params=pltpu.CompilerParams(
            collective_id=0, has_side_effects=True, vmem_limit_bytes=56 * 1024 * 1024
        ),
        cost_estimate=pl.CostEstimate(
            flops=20_000_000_000, bytes_accessed=12_000_000, transcendentals=11_000_000
        ),
    )(doc_lengths, inverse, queries, key_heads, token_value_heads, out_weight)


def solution(mesh):
    return jax.shard_map(
        body,
        mesh=mesh,
        in_specs=(P("seq", "tp"), P("seq", "tp"), P("seq", "tp"), P("tp", None), P(), P()),
        out_specs=P("seq", "tp"),
        check_vma=False,
    )
```

time: 168 us -> 130 us (0.77)
  the two profiles are of different devices: /device:TPU:63 before, /device:TPU:2 now
where the time goes in v2:
time: 130 us
  Pallas kernels  126 us (97%)
  local copies, waits for them, and re-layouts  2.49 us (2%)
  other arithmetic  1.52 us (1%)
    pallas_call x1, Pallas kernels, body(): pl.pallas_call(kernel, out_shape=jax.ShapeDtypeStruct((ROWS, WIDTH), bf16...  126 us

profile of v2, /device:TPU:2, one launch (start us, length us, event | category | flops | bytes accessed | tf_op | source)
XLA Modules:
  0.0 130.0 jit_solution(6400917395223989853)
XLA Ops:
  0.0 0.7 iota_compare_fusion
  0.7 0.8 select_reduce_fusion.inverse_ref
  1.5 126.0 %shard_map.64 = bf16[1024,640]{1,0:T(8,128)(2,1)} custom-call(s32[8,12]{1,0:T(8,128)} %doc_ref.1, s32[8,32]{1,0:T(8,128)} %select_reduce_fusion.inverse_ref, bf16[1024,640]{1,0:T(8,128)(2,1)} %q_ref.1, bf16[1024,128]{1,0:T(8,128)(2,1)} %k_hbm.1, bf16[1024,128]{1,0:T(8,128)(2,1)} %v_hbm.1, bf16[640,5120]{1,0:T(8,128)(2,1)} %w_hbm.1), custom_call_target="tpu_custom_call" | custom-call | flops 20000000000 | bytes 12000000 | tf_op jit(solution)/shard_map/pallas_call | solution.py:575
  127.5 2.5 %copy.8 = bf16[1024,640]{1,0:T(8,128)(2,1)} copy(bf16[1024,640]{1,0:T(8,128)(2,1)} %shard_map.64) | data formatting | bytes 2621440
  (3 shorter events, 0.0 us)

commit v3 on v2

--- a/solution.py
+++ b/solution.py
@@ -59,14 +59,18 @@
 
 def kernel(
     doc_ref,
-    inverse_ref,
-    q_ref,
+    owner_ref,
+    q_hbm,
     k_hbm,
     v_hbm,
     w_hbm,
     out_ref,
+    queries,
     kbuf,
     vbuf,
+    probs,
+    inverse_vmem,
+    inverse_ref,
     weight,
     att,
     psend,
@@ -119,7 +123,9 @@
 
     own_k = pltpu.make_async_copy(k_hbm, kbuf.at[pl.ds(2 * ROWS, ROWS)], local_sem.at[0])
     own_v = pltpu.make_async_copy(v_hbm, vbuf.at[pl.ds(2 * ROWS, ROWS)], local_sem.at[1])
+    own_q = pltpu.make_async_copy(q_hbm, queries, local_sem.at[4])
     own_k.start()
+    own_q.start()
     own_v.start()
 
     def own_weight(half):
@@ -143,6 +149,19 @@
 
     for target in (pair, buddy, far, far_buddy):
         pl.semaphore_signal(barrier, inc=1, device_id={"tp": target}, device_id_type=MESH)
+
+    block_no = lax.broadcasted_iota(jnp.int32, (8, 128), 0)
+    owner_no = lax.broadcasted_iota(jnp.int32, (8, 128), 1)
+
+    def add_index(index, inverse):
+        for block in range(BLOCKS):
+            here = (block_no == block) & (owner_no == owner_ref[index * BLOCKS + block])
+            inverse = jnp.where(here, index, inverse)
+        return inverse
+
+    inverse_vmem[...] = lax.fori_loop(0, SEQ, add_index, jnp.zeros((8, 128), jnp.int32))
+    to_scalars = pltpu.make_async_copy(inverse_vmem, inverse_ref, local_sem.at[5])
+    to_scalars.start()
     pl.semaphore_wait(barrier, SEQ - 1 + 4)
 
     piece_no = (core * 4 + y) * 4 + x
@@ -220,15 +239,18 @@
             {"seq": lax.rem(me + 2, SEQ)},
         )
 
-    @pl.when(j < 3)
-    def _():
-        near_kv(0).start()
-        near_kv(1).start()
+    for which in range(2):
+
+        @pl.when(j < 3)
+        def _():
+            near_kv(which).start()
+
+        @pl.when(j < 2)
+        def _():
+            next_kv(which, BLOCKS - 1).start()
 
     @pl.when(j < 2)
     def _():
-        next_kv(0, BLOCKS - 1).start()
-        next_kv(1, BLOCKS - 1).start()
         kbuf[pl.ds(0, ROWS), :] = jnp.zeros((ROWS, HEAD_SIZE), kbuf.dtype)
         vbuf[pl.ds(0, ROWS), :] = jnp.zeros((ROWS, HEAD_SIZE), vbuf.dtype)
 
@@ -242,6 +264,11 @@
 
     def slot(no):
         return pl.ds(no * WIDTH, WIDTH)
+
+    def span(place, part):
+        if part is None:
+            return rows_of(place), place
+        return pl.ds((BLOCKS - 1) * BLK + part * (BLK // 2), BLK // 2), BLOCKS - 1 + part
 
     def own_copy(block):
         rows = rows_of(block)
@@ -253,38 +280,51 @@
             {"tp": buddy},
         )
 
-    def far_copy(block):
-        rows = rows_of(block)
+    def far_copy(place, part=None):
+        rows, sem = span(place, part)
         return remote(
             att.at[rows, slot(0)],
             att.at[rows, slot(2)],
-            far_send.at[block],
-            far_recv.at[block],
+            far_send.at[sem],
+            far_recv.at[sem],
             {"tp": far},
         )
 
-    def forward_copy(block):
-        rows = rows_of(block)
+    def forward_copy(place, part=None):
+        rows, sem = span(place, part)
         return remote(
             att.at[rows, slot(2)],
             att.at[rows, slot(3)],
-            forward_send.at[block],
-            forward_recv.at[block],
+            forward_send.at[sem],
+            forward_recv.at[sem],
             {"tp": buddy},
         )
 
-    def pair_copy(block):
-        rows = rows_of(block)
-        return remote(
-            psend.at[rows], precv.at[rows], pair_send.at[block], pair_recv.at[block], {"tp": pair}
-        )
-
-    def attention(place):
+    def pair_copy(place, part=None):
+        rows, sem = span(place, part)
+        return remote(
+            psend.at[rows], precv.at[rows], pair_send.at[sem], pair_recv.at[sem], {"tp": pair}
+        )
+
+    def wait_kv(step, block, which):
+        @pl.when(step == 0)
+        def _():
+            (own_k, own_v)[which].wait()
+
+        @pl.when((step == 0) & (j >= 1))
+        def _():
+            near_kv(which).wait_recv()
+
+        @pl.when(j >= 2)
+        def _():
+            next_kv(which, block).wait_recv()
+
+    def attention(step, place):
         block = block_at(place)
         rows = rows_of(block)
         window = pl.ds(pl.multiple_of(block * BLK, BLK), WINDOW)
+        wait_kv(step, block, 0)
         keys = kbuf[window, :]
-        values = vbuf[window, :]
         base = j * ROWS + block * BLK
         position = base + lax.broadcasted_iota(jnp.int32, (BLK, 1), 0)
         bound = jnp.int32(0)
@@ -296,25 +336,29 @@
         key_no = lax.broadcasted_iota(jnp.int32, (BLK, WINDOW), 1)
         last = MAXDOC + lax.broadcasted_iota(jnp.int32, (BLK, WINDOW), 0)
         allowed = (key_no >= first) & (key_no <= last)
+        totals = []
         for head in range(HEADS):
             columns = pl.ds(head * HEAD_SIZE, HEAD_SIZE)
             scores = lax.dot_general(
-                q_ref[rows, columns],
+                queries[rows, columns],
                 keys,
                 (((1,), (1,)), ((), ())),
                 preferred_element_type=jnp.float32,
             )
             scores = jnp.where(allowed, scores * scale, -1e30)
             weights = jnp.exp2(scores - jnp.max(scores, axis=1, keepdims=True))
-            total = jnp.sum(weights, axis=1, keepdims=True)
-            mix = jnp.dot(
-                weights.astype(jnp.bfloat16), values, preferred_element_type=jnp.float32
-            )
-            attended[rows_of(place), columns] = (mix / total).astype(jnp.bfloat16)
-
-    def project(block, half):
+            totals.append(jnp.sum(weights, axis=1, keepdims=True))
+            probs[pl.ds(head * BLK, BLK), :] = weights.astype(jnp.bfloat16)
+        wait_kv(step, block, 1)
+        mix = jnp.dot(probs[...], vbuf[window, :], preferred_element_type=jnp.float32)
+        for head in range(HEADS):
+            part = mix[head * BLK : (head + 1) * BLK] / totals[head]
+            columns = pl.ds(head * HEAD_SIZE, HEAD_SIZE)
+            attended[rows_of(place), columns] = part.astype(jnp.bfloat16)
+
+    def project(rows, half):
         return jnp.dot(
-            att[rows_of(block), :],
+            att[rows, :],
             weight[pl.ds(0, 4 * WIDTH), pl.ds(half * WIDTH, WIDTH)],
             preferred_element_type=jnp.float32,
         )
@@ -391,22 +435,28 @@
         ref = att.at[rows_of(place), slot(0)]
         pltpu.make_async_copy(ref, ref, placed_recv.at[place - HALF]).wait()
 
-    def own_result(place):
+    def own_result(place, part=None):
+        rows = span(place, part)[0]
+        if part is None:
+            out_rows = rows_of(block_at(place))
+        else:
+            out_rows = pl.ds(part * (BLK // 2), BLK // 2)
         return pltpu.make_async_copy(
-            mixed.at[rows_of(place)], out_ref.at[rows_of(block_at(place))], out_recv.at[place]
-        )
+            mixed.at[rows], out_ref.at[out_rows], out_recv.at[place]
+        )
+
+    def parts_of(place):
+        return [
+            lambda f: pl.when(place < BLOCKS - 1)(lambda: f(None)),
+            lambda f: pl.when(place == BLOCKS - 1)(lambda: (f(0), f(1))[0]),
+        ]
 
     @pl.loop(0, BLOCKS + D_FINAL)
     def _(step):
         @pl.when(step == 0)
         def _():
-            own_k.wait()
-            own_v.wait()
-
-            @pl.when(j >= 1)
-            def _():
-                near_kv(0).wait_recv()
-                near_kv(1).wait_recv()
+            own_q.wait()
+            to_scalars.wait()
 
         @pl.when(step == 1)
         def _():
@@ -442,13 +492,22 @@
         @pl.when((step >= D_FORWARD) & (step < D_FORWARD + BLOCKS))
         def _():
             place = step - D_FORWARD
-            far_copy(place).wait_recv()
-            forward_copy(place).start()
+            for part in parts_of(place):
+
+                @part
+                def _(number):
+                    far_copy(place, number).wait_recv()
+                    forward_copy(place, number).start()
 
         @pl.when((step >= HALF) & (step < BLOCKS))
         def _():
             placed_wait(step)
-            far_copy(step).start()
+            for part in parts_of(step):
+
+                @part
+                def _(number):
+                    far_copy(step, number).start()
+
             own_copy(step).start()
 
         @pl.loop(0, 2)
@@ -458,12 +517,7 @@
 
             @pl.when((step >= first_step) & (step < first_step + HALF))
             def _():
-                @pl.when(j >= 2)
-                def _():
-                    next_kv(0, block_at(place)).wait_recv()
-                    next_kv(1, block_at(place)).wait_recv()
-
-                attention(place)
+                attention(step, place)
 
                 @pl.when(late == 0)
                 def _():
@@ -487,29 +541,39 @@
         @pl.when((step >= D_PROJ) & (step < D_PROJ + BLOCKS))
         def _():
             place = step - D_PROJ
+            own_copy(place).wait_recv()
+            for part in parts_of(place):
+
+                @part
+                def _(number):
+                    rows = span(place, number)[0]
+                    forward_copy(place, number).wait_recv()
+                    psend[rows, :] = project(rows, 1).astype(jnp.bfloat16)
+                    pair_copy(place, number).start()
+
             rows = rows_of(place)
-            own_copy(place).wait_recv()
-            forward_copy(place).wait_recv()
-            psend[rows, :] = project(place, 1).astype(jnp.bfloat16)
-            pair_copy(place).start()
-            own_part[rows, :] = project(place, 0)
+            own_part[rows, :] = project(rows, 0)
 
         @pl.when((step >= D_FINAL) & (step < D_FINAL + BLOCKS))
         def _():
             place = step - D_FINAL
-            rows = rows_of(place)
-            pair_copy(place).wait_recv()
-            mixed[rows, :] = (
-                own_part[rows, :] + precv[rows, :].astype(jnp.float32)
-            ).astype(jnp.bfloat16)
+            for part in parts_of(place):
+
+                @part
+                def _(number):
+                    rows = span(place, number)[0]
+                    pair_copy(place, number).wait_recv()
+                    mixed[rows, :] = (
+                        own_part[rows, :] + precv[rows, :].astype(jnp.float32)
+                    ).astype(jnp.bfloat16)
+
+                    @pl.when(place >= HALF)
+                    def _():
+                        own_result(place, number).start()
 
             @pl.when(place < HALF)
             def _():
                 route(place, 0)
-
-            @pl.when(place >= HALF)
-            def _():
-                own_result(place).start()
 
         reorder(step - D_MID, 0)
 
@@ -539,9 +603,14 @@
     @pl.loop(0, BLOCKS)
     def _(block):
         own_copy(block).wait_send()
-        far_copy(block).wait_send()
-        forward_copy(block).wait_send()
-        pair_copy(block).wait_send()
+        for part in parts_of(block):
+
+            @part
+            def _(number):
+                far_copy(block, number).wait_send()
+                forward_copy(block, number).wait_send()
+                pair_copy(block, number).wait_send()
+
         for piece in range(PIECES):
             target = middle_of(block, piece)
 
@@ -558,28 +627,22 @@
 
 
 def body(queries, key_heads, token_value_heads, out_weight, doc_lengths, owner_of):
-    index = jnp.arange(SEQ * BLOCKS, dtype=jnp.int32)[None, None, :]
-    blocks = jnp.arange(BLOCKS, dtype=jnp.int32)[:, None, None]
-    owners = jnp.arange(SEQ, dtype=jnp.int32)[None, :, None]
-    inverse = jnp.sum(
-        jnp.where(
-            (owner_of[None, None, :] == owners) & (index % BLOCKS == blocks), index // BLOCKS, 0
-        ),
-        axis=2,
-    )
     dma = pltpu.SemaphoreType.DMA
     bf16 = jnp.bfloat16
     any_space = pl.BlockSpec(memory_space=pl.ANY)
     smem = pl.BlockSpec(memory_space=pltpu.SMEM)
-    vmem = pl.BlockSpec(memory_space=pltpu.VMEM)
     return pl.pallas_call(
         kernel,
         out_shape=jax.ShapeDtypeStruct((ROWS, WIDTH), bf16),
-        in_specs=[smem, smem, vmem, any_space, any_space, any_space],
+        in_specs=[smem, smem] + [any_space] * 4,
         out_specs=any_space,
         scratch_shapes=[
+            pltpu.VMEM((ROWS, WIDTH), bf16),
             pltpu.VMEM((3 * ROWS, HEAD_SIZE), bf16),
             pltpu.VMEM((3 * ROWS, HEAD_SIZE), bf16),
+            pltpu.VMEM((HEADS * BLK, WINDOW), bf16),
+            pltpu.VMEM((8, 128), jnp.int32),
+            pltpu.SMEM((8, 128), jnp.int32),
             pltpu.VMEM((W_ROWS, 2 * WIDTH), bf16),
             pltpu.VMEM((ROWS, 4 * WIDTH), bf16),
             pltpu.VMEM((ROWS, WIDTH), bf16),
@@ -590,19 +653,19 @@
             pltpu.VMEM((SEQ, PIECE, WIDTH), bf16),
             pltpu.VMEM((SEQ, PIECE, WIDTH), bf16),
             pltpu.VMEM((2, SEQ, PIECE, WIDTH), bf16),
-            dma((4,)),
+            dma((6,)),
             dma((2, BLOCKS + 1)),
             dma((2, BLOCKS + 1)),
             dma((16,)),
             dma((16,)),
             dma((BLOCKS,)),
             dma((BLOCKS,)),
-            dma((BLOCKS,)),
-            dma((BLOCKS,)),
-            dma((BLOCKS,)),
-            dma((BLOCKS,)),
-            dma((BLOCKS,)),
-            dma((BLOCKS,)),
+            dma((BLOCKS + 1,)),
+            dma((BLOCKS + 1,)),
+            dma((BLOCKS + 1,)),
+            dma((BLOCKS + 1,)),
+            dma((BLOCKS + 1,)),
+            dma((BLOCKS + 1,)),
             dma((BLOCKS, PIECES)),
             dma((2,)),
             dma((2, SEQ)),
@@ -615,7 +678,7 @@
         cost_estimate=pl.CostEstimate(
             flops=20_000_000_000, bytes_accessed=12_000_000, transcendentals=11_000_000
         ),
-    )(doc_lengths, inverse, queries, key_heads, token_value_heads, out_weight)
+    )(doc_lengths, owner_of, queries, key_heads, token_value_heads, out_weight)
 
 
 def solution(mesh):

time: 130 us -> 126 us (0.969)
  Pallas kernels: 126 us -> 124 us
  other arithmetic: 1.52 us -> 0 us
    pallas_call x1, Pallas kernels: 126 us -> 124 us  [body(): pl.pallas_call(kernel, out_shape=jax.ShapeDtypeStruct((ROWS, WIDTH), bf16...]
where the time goes in v3:
time: 126 us
  Pallas kernels  124 us (98%)
  local copies, waits for them, and re-layouts  2.49 us (2%)
    pallas_call x1, Pallas kernels, body(): pl.pallas_call(kernel, out_shape=jax.ShapeDtypeStruct((ROWS, WIDTH), bf16...  124 us

profile of v3, /device:TPU:2, one launch (start us, length us, event | category | flops | bytes accessed | tf_op | source)
XLA Modules:
  0.0 126.2 jit_solution(7660946839460571740)
XLA Ops:
  0.0 123.7 %shard_map.64 = bf16[1024,640]{1,0:T(8,128)(2,1)} custom-call(s32[8,12]{1,0:T(8,128)} %doc_ref.1, s32[256]{0:T(256)} %owner_ref.1, bf16[1024,640]{1,0:T(8,128)(2,1)} %q_hbm.1, bf16[1024,128]{1,0:T(8,128)(2,1)} %k_hbm.1, bf16[1024,128]{1,0:T(8,128)(2,1)} %v_hbm.1, bf16[640,5120]{1,0:T(8,128)(2,1)} %w_hbm.1), custom_call_target="tpu_custom_call" | custom-call | flops 20000000000 | bytes 12000000 | tf_op jit(solution)/shard_map/pallas_call | solution.py:634
  123.7 2.5 %copy.8 = bf16[1024,640]{1,0:T(8,128)(2,1)} copy(bf16[1024,640]{1,0:T(8,128)(2,1)} %shard_map.64) | data formatting | bytes 2621440

commit v4 on v3

--- a/solution.py
+++ b/solution.py
@@ -28,10 +28,10 @@
 
 HALF = BLOCKS // 2
 
-D_FORWARD = 2
-D_PROJ = 4
-D_FINAL = 5
-D_MID = 6
+D_FORWARD = 1
+D_PROJ = 3
+D_FINAL = 4
+D_MID = 5
 
 
 def block_at(place):
@@ -215,8 +215,8 @@
         ref = weight.at[rows, w_half(half)]
         return remote(ref, ref, w_send.at[sem], w_recv.at[sem], {"seq": me + 1 - 2 * core})
 
+    w_first(1).start()
     w_first(0).start()
-    w_first(1).start()
 
     def near_kv(which):
         src, buf = ((k_hbm, kbuf), (v_hbm, vbuf))[which]
@@ -460,7 +460,7 @@
 
         @pl.when(step == 1)
         def _():
-            for half in range(2):
+            for half in (1, 0):
                 w_first(half).wait_recv()
                 for hop in (1, 3, 2):
                     w_second(half, hop).start()
@@ -474,30 +474,15 @@
 
         @pl.when(step == 2)
         def _():
-            for half in range(2):
-                for hop in (1, 3, 2):
-                    w_second(half, hop).wait_recv()
+            for hop in (1, 3, 2):
+                w_second(1, hop).wait_recv()
+            for hop in (1, 3, 2):
+                for yy in range(4):
+                    w_third_piece(hop, yy).start()
+            for hop in (1, 3, 2):
+                w_second(0, hop).wait_recv()
             for hop in (1, 3, 2):
                 w_third(0, hop).start()
-                for yy in range(4):
-                    w_third_piece(hop, yy).start()
-
-        @pl.when(step == 3)
-        def _():
-            for half in range(2):
-                for hop in (1, 3, 2):
-                    w_third(half, hop).wait_recv()
-                w_fourth(half).start()
-
-        @pl.when((step >= D_FORWARD) & (step < D_FORWARD + BLOCKS))
-        def _():
-            place = step - D_FORWARD
-            for part in parts_of(place):
-
-                @part
-                def _(number):
-                    far_copy(place, number).wait_recv()
-                    forward_copy(place, number).start()
 
         @pl.when((step >= HALF) & (step < BLOCKS))
         def _():
@@ -530,13 +515,29 @@
                 def _():
                     route(place, 1)
 
+        @pl.when((step >= D_FORWARD) & (step < D_FORWARD + BLOCKS))
+        def _():
+            place = step - D_FORWARD
+            for part in parts_of(place):
+
+                @part
+                def _(number):
+                    far_copy(place, number).wait_recv()
+                    forward_copy(place, number).start()
+
+        @pl.when(step == 3)
+        def _():
+            for half in (1, 0):
+                for hop in (1, 3, 2):
+                    w_third(half, hop).wait_recv()
+                w_fourth(half).start()
+
         reorder(step + 2, 1)
 
         @pl.when(step == D_PROJ)
         def _():
-            for half in range(2):
-                own_weight(half).wait()
-                w_fourth(half).wait_recv()
+            own_weight(1).wait()
+            w_fourth(1).wait_recv()
 
         @pl.when((step >= D_PROJ) & (step < D_PROJ + BLOCKS))
         def _():
@@ -550,6 +551,11 @@
                     forward_copy(place, number).wait_recv()
                     psend[rows, :] = project(rows, 1).astype(jnp.bfloat16)
                     pair_copy(place, number).start()
+
+            @pl.when(place == 0)
+            def _():
+                own_weight(0).wait()
+                w_fourth(0).wait_recv()
 
             rows = rows_of(place)
             own_part[rows, :] = project(rows, 0)

time: 126 us -> 121 us (0.960)
  Pallas kernels: 124 us -> 118 us
    pallas_call x1, Pallas kernels: 124 us -> 118 us  [body(): pl.pallas_call(kernel, out_shape=jax.ShapeDtypeStruct((ROWS, WIDTH), bf16...]
where the time goes in v4:
time: 121 us; the launch traced here: 120 us
  Pallas kernels  118 us (98%)
  local copies, waits for them, and re-layouts  2.49 us (2%)
    pallas_call x1, Pallas kernels, body(): pl.pallas_call(kernel, out_shape=jax.ShapeDtypeStruct((ROWS, WIDTH), bf16...  118 us
    unnamed x1, local copies, waits for them, and re-layouts  2.49 us

profile of v4, /device:TPU:2, one launch (start us, length us, event | category | flops | bytes accessed | tf_op | source)
XLA Modules:
  0.0 120.3 jit_solution(6056065260527031749)
XLA Ops:
  0.0 117.8 %shard_map.64 = bf16[1024,640]{1,0:T(8,128)(2,1)} custom-call(s32[8,12]{1,0:T(8,128)} %doc_ref.1, s32[256]{0:T(256)} %owner_ref.1, bf16[1024,640]{1,0:T(8,128)(2,1)} %q_hbm.1, bf16[1024,128]{1,0:T(8,128)(2,1)} %k_hbm.1, bf16[1024,128]{1,0:T(8,128)(2,1)} %v_hbm.1, bf16[640,5120]{1,0:T(8,128)(2,1)} %w_hbm.1), custom_call_target="tpu_custom_call" | custom-call | flops 20000000000 | bytes 12000000 | tf_op jit(solution)/shard_map/pallas_call | solution.py:640
  117.8 2.5 %copy.8 = bf16[1024,640]{1,0:T(8,128)(2,1)} copy(bf16[1024,640]{1,0:T(8,128)(2,1)} %shard_map.64) | data formatting | bytes 2621440

commit v5 on v4

--- a/solution.py
+++ b/solution.py
@@ -30,8 +30,8 @@
 
 D_FORWARD = 1
 D_PROJ = 3
-D_FINAL = 4
-D_MID = 5
+D_FINAL = 5
+D_MID = 6
 
 
 def block_at(place):

time: 121 us -> 121 us (level); the launches traced: 120 us -> 119 us
  Pallas kernels: 118 us -> 116 us
    pallas_call x1, Pallas kernels: 118 us -> 116 us  [body(): pl.pallas_call(kernel, out_shape=jax.ShapeDtypeStruct((ROWS, WIDTH), bf16...]
where the time goes in v5:
time: 121 us; the launch traced here: 119 us
  Pallas kernels  116 us (96%)
  local copies, waits for them, and re-layouts  2.49 us (2%)
    pallas_call x1, Pallas kernels, body(): pl.pallas_call(kernel, out_shape=jax.ShapeDtypeStruct((ROWS, WIDTH), bf16...  116 us
    unnamed x1, local copies, waits for them, and re-layouts  2.49 us

profile of v5, /device:TPU:2, one launch (start us, length us, event | category | flops | bytes accessed | tf_op | source)
XLA Modules:
  0.0 119.0 jit_solution(11412435827600803941)
XLA Ops:
  0.0 116.5 %shard_map.64 = bf16[1024,640]{1,0:T(8,128)(2,1)} custom-call(s32[8,12]{1,0:T(8,128)} %doc_ref.1, s32[256]{0:T(256)} %owner_ref.1, bf16[1024,640]{1,0:T(8,128)(2,1)} %q_hbm.1, bf16[1024,128]{1,0:T(8,128)(2,1)} %k_hbm.1, bf16[1024,128]{1,0:T(8,128)(2,1)} %v_hbm.1, bf16[640,5120]{1,0:T(8,128)(2,1)} %w_hbm.1), custom_call_target="tpu_custom_call" | custom-call | flops 20000000000 | bytes 12000000 | tf_op jit(solution)/shard_map/pallas_call | solution.py:640
  116.5 2.5 %copy.8 = bf16[1024,640]{1,0:T(8,128)(2,1)} copy(bf16[1024,640]{1,0:T(8,128)(2,1)} %shard_map.64) | data formatting | bytes 2621440
